TPU v7x, 128 devices: a whole 4x4x4 slice. The times are simulated.
128 devices in a mesh: ta: 16 (over z_hi, y, core), sa: 8 (over z_lo, x).
Axes of the slice: x: 4, y: 4, z: 4 (z_hi: 2, z_lo: 2; z = z_hi * 2 + z_lo), core: 2. Of those that a mesh axis runs over, the one named last changes fastest.
Arguments:
- video_q: bfloat16 [16, 8, 256, 3072], P('ta', 'sa'), may hold values from -120 to 120
- video_kv: bfloat16 [16, 8, 256, 6144], P('ta', 'sa'), may hold values from -6 to 6
- text_qkv: bfloat16 [256, 9216], P(('ta', 'sa')), may hold values from -120 to 120
- text_mask: int32 [256], replicated, may hold values 0 or 1
- pattern: int32 [16, 8, 4], P('ta', 'sa'), may hold values from -1 to 127, as said below
Outputs:
- video_out: bfloat16 [16, 8, 256, 3072], P('ta', 'sa')
- text_out: bfloat16 [256, 3072], P(('ta', 'sa'))
Inputs may be any that keep to these rules, and one draw needn't show every extreme that they name: `pattern`: for tile (t, s) the row lists distinct indices of the tile itself (always first) and of tiles one step away along time or along space, then -1 in unused slots; it lists 1 to 4 tiles, and in every draw some tiles list 4.
All inputs are finite; a program needn't handle non-finite values.
Results may differ from a plain program's by a relative error of at most 0.03.
Values may be sent and summed in bfloat16 or wider, within the bound.
A program may use at most 768 MiB of HBM per device.

v0:
```python
import math

import jax
import jax.numpy as jnp
from jax import lax
from jax.sharding import PartitionSpec as P

HEAD = 128


def from_behind(block, axis, distance):
    devices = range(lax.axis_size(axis))
    route = [(i - distance, i) for i in devices if i - distance in devices]
    return lax.ppermute(block, axis, route)


def attend(query, key_rows, value_rows, is_valid):
    head_count = query.shape[1] // HEAD
    scale = 1.0 / math.sqrt(HEAD)

    def attend_one_head(head_index):
        first_col = head_index * HEAD
        q_part = lax.dynamic_slice_in_dim(query, first_col, HEAD, 1)
        k_part = lax.dynamic_slice_in_dim(key_rows, first_col, HEAD, 1)
        v_part = lax.dynamic_slice_in_dim(value_rows, first_col, HEAD, 1)
        scores = (
            lax.dot_general(
                q_part, k_part, (((1,), (1,)), ((), ())), preferred_element_type=jnp.float32
            )
            * scale
        )
        scores = jnp.where(is_valid[None, :], scores, -1e30)
        row_top = jnp.max(scores, axis=1, keepdims=True)
        weights = jnp.exp(scores - row_top)
        row_total = jnp.sum(weights, axis=1, keepdims=True)
        mixed = jnp.dot(weights.astype(jnp.bfloat16), v_part, preferred_element_type=jnp.float32)
        return mixed / row_total

    stacked = lax.map(attend_one_head, jnp.arange(head_count, dtype=jnp.int32))
    return (
        jnp.transpose(stacked, (1, 0, 2))
        .reshape(query.shape[0], head_count * HEAD)
        .astype(jnp.bfloat16)
    )


def partial_softmax(query, key_rows, value_rows, is_valid):
    head_count = query.shape[1] // HEAD
    scale = 1.0 / math.sqrt(HEAD)

    def partial_one_head(head_index):
        first_col = head_index * HEAD
        q_part = lax.dynamic_slice_in_dim(query, first_col, HEAD, 1)
        k_part = lax.dynamic_slice_in_dim(key_rows, first_col, HEAD, 1)
        v_part = lax.dynamic_slice_in_dim(value_rows, first_col, HEAD, 1)
        scores = (
            lax.dot_general(
                q_part, k_part, (((1,), (1,)), ((), ())), preferred_element_type=jnp.float32
            )
            * scale
        )
        scores = jnp.where(is_valid[None, :], scores, -1e30)
        row_top = jnp.max(scores, axis=1)
        weights = jnp.exp(scores - row_top[:, None])
        row_total = jnp.sum(weights, axis=1)
        mixed = jnp.dot(weights.astype(jnp.bfloat16), v_part, preferred_element_type=jnp.float32)
        return (row_top, row_total, mixed)

    return lax.map(partial_one_head, jnp.arange(head_count, dtype=jnp.int32))


def combine(first, second):
    joint_top = jnp.maximum(first[0], second[0])
    scale_one = jnp.exp(first[0] - joint_top)
    scale_two = jnp.exp(second[0] - joint_top)
    row_total = first[1] * scale_one + second[1] * scale_two
    mixed = first[2] * scale_one[..., None] + second[2] * scale_two[..., None]
    return (joint_top, row_total, mixed)


def local(video_q, video_kv, text_qkv, text_mask, pattern):
    tile_len = video_q.shape[2]
    model_width = video_q.shape[3]
    space_count = lax.axis_size("sa")
    time_here = lax.axis_index("ta")
    space_here = lax.axis_index("sa")
    gathered = lax.all_gather(text_qkv, ("ta", "sa"), axis=0, tiled=True)
    text_keys = gathered[:, model_width : 2 * model_width]
    text_values = gathered[:, 2 * model_width :]
    text_valid = text_mask == 1
    own_kv = video_kv[0, 0]
    time_earlier = from_behind(own_kv, "ta", 1)
    time_later = from_behind(own_kv, "ta", -1)
    space_left = from_behind(own_kv, "sa", 1)
    space_right = from_behind(own_kv, "sa", -1)
    kv_stack = jnp.stack([own_kv, time_earlier, time_later, space_left, space_right])
    tile_row = pattern[0, 0]
    time_step = tile_row // space_count - time_here
    space_step = tile_row % space_count - space_here
    slot_index = jnp.where(
        time_step == -1,
        1,
        jnp.where(
            time_step == 1, 2, jnp.where(space_step == -1, 3, jnp.where(space_step == 1, 4, 0))
        ),
    )
    chosen = jnp.take(kv_stack, slot_index, axis=0).reshape(-1, 2 * model_width)
    key_rows = jnp.concatenate([chosen[:, :model_width], text_keys], axis=0)
    value_rows = jnp.concatenate([chosen[:, model_width:], text_values], axis=0)
    is_valid = jnp.concatenate([jnp.repeat(tile_row >= 0, tile_len), text_valid])
    video_out = attend(video_q[0, 0], key_rows, value_rows, is_valid)[None, None]
    own_valid = jnp.ones((tile_len,), dtype=bool)
    tops, totals, mixes = partial_softmax(
        gathered[:, :model_width], own_kv[:, :model_width], own_kv[:, model_width:], own_valid
    )
    own_rows = text_qkv.shape[0]
    row_start = lax.axis_index(("ta", "sa")) * own_rows
    global_peak = lax.pmax(tops, ("ta", "sa"))
    factor = jnp.exp(tops - global_peak)
    video_total, video_mix = (
        lax.psum_scatter(totals * factor, ("ta", "sa"), scatter_dimension=1, tiled=True),
        lax.psum_scatter(mixes * factor[..., None], ("ta", "sa"), scatter_dimension=1, tiled=True),
    )
    video_top = lax.dynamic_slice_in_dim(global_peak, row_start, own_rows, 1)
    text_top, text_total, text_mix = partial_softmax(
        text_qkv[:, :model_width], text_keys, text_values, text_valid
    )
    joint = combine((video_top, video_total, video_mix), (text_top, text_total, text_mix))
    text_heads = joint[2] / joint[1][..., None]
    text_out = (
        jnp.transpose(text_heads, (1, 0, 2)).reshape(own_rows, model_width).astype(jnp.bfloat16)
    )
    return (video_out, text_out)


def solution(mesh):
    in_specs = (
        P("ta", "sa", None, None),
        P("ta", "sa", None, None),
        P(("ta", "sa"), None),
        P(),
        P("ta", "sa", None),
    )
    out_specs = (P("ta", "sa", None, None), P(("ta", "sa"), None))
    return jax.shard_map(local, mesh=mesh, in_specs=in_specs, out_specs=out_specs, check_vma=False)
```

profile of v0, /device:TPU:0, one launch (start us, length us, event | category | flops | bytes accessed | tf_op | source)
XLA Modules:
  0.0 1391.4 jit_solution(7999792247982269174)
XLA Ops:
  11.8 5.6 collective-permute-start.2
  35.8 49.3 %collective-permute-done.2 = bf16[256,6144]{1,0:T(8,128)(2,1)} collective-permute-done((bf16[256,6144]{1,0:T(8,128)(2,1)}, bf16[256,6144]{1,0:T(8,128)(2,1)}, u32[]{:S(2)}, u32[]{:S(2)}) %collective-permute-start.2) | collective-permute-done | bytes 3145760 | tf_op jit(solution)/shard_map/ppermute | solution.py:14
  95.3 11.0 fusion.45
  106.3 6.8 gather_fusion
  113.1 6.8 gather_fusion.1
  120.0 6.2 pad_maximum_fusion
  128.4 5.4 fusion.46
  133.8 269.6 %all-gather.3.cloned.1.call-done = bf16[128,2,9216]{2,1,0:T(2,128)(2,1)} async-done(((bf16[1,2,9216]{2,1,0:T(2,128)(2,1)}), bf16[128,2,9216]{2,1,0:T(2,128)(2,1)}) %all-gather.3.cloned.1.call-update) | async-done | bytes 4718608 | tf_op jit(solution)/shard_map/all_gather | solution.py:87
  403.4 7.5 reshape.189
  414.8 259.5 %while.39 = (s32[]{:T(128)}, f32[24,256]{1,0:T(8,128)}, f32[24,256]{1,0:T(8,128)}, f32[24,256,128]{2,0,1:T(8,128)}, s32[24]{0:T(128)S(1)}, /*index=5*/bf16[256,3...) while((s32[]{:T(128)}, f32[24,256]{1,0:T(8,128)}, ...), condition=%wide.region_7.8_spmd, body=%wide.region_4.7_spmd.sunk | while | flops 33947140 | bytes 1385663 | solution.py:69
  418.2 4.7 dynamic_update_slice.36
  429.1 4.7 dynamic_update_slice.36
  439.9 4.7 dynamic_update_slice.36
  450.7 4.7 dynamic_update_slice.36
  461.5 4.7 dynamic_update_slice.36
  472.4 4.7 dynamic_update_slice.36
  483.2 4.7 dynamic_update_slice.36
  494.0 4.7 dynamic_update_slice.36
  674.3 63.6 %pmax.7 = f32[24,256]{1,0:T(8,128)S(1)} all-reduce(f32[24,256]{1,0:T(8,128)} %get-tuple-element.134), channel_id=1, replica_groups=mesh['ta'=16,'sa'=8] {'ta','sa'}, use_global_device_ids=true, to_apply=%region_8.9 | all-reduce | flops 6144 | bytes 49152 | tf_op jit(solution)/shard_map/pmax | solution.py:118
  742.4 10.8 pad_maximum_fusion.1
  753.2 123.6 %while.38 = (s32[]{:T(128)}, bf16[24,256,128]{2,1,0:T(8,128)(2,1)}, pred[1280]{0:T(1024)(128)(4,1)S(1)}, s32[24]{0:T(128)S(1)}, bf16[256,3072]{1,0:T(8,128)(2,1)...) while((s32[]{:T(128)}, bf16[24,256,128]{2,1,0:T(8,128)(2,1)}, ...), condition=%wide.region_3.4_spmd, body=%wide.region_0.3_spmd.sunk | while | flops 170098176 | bytes 4792235 | solution.py:39
  876.8 94.1 %while.40 = (s32[]{:T(128)}, f32[24,2]{1,0:T(8,128)S(1)}, f32[24,2]{1,0:T(8,128)S(1)}, f32[24,2,128]{2,0,1:T(8,128)}, pred[256]{0:T(512)(128)(4,1)S(1)}, /*index...) while((s32[]{:T(128)}, f32[24,2]{1,0:T(8,128)S(1)}, ...), condition=%wide.region_13.14_spmd, body=%wide.region_10.13_spmd.sunk | while | flops 265730 | bytes 143103 | solution.py:69
  970.9 64.5 %all-reduce = f32[24,256]{1,0:T(8,128)S(1)} all-reduce(f32[24,256]{1,0:T(8,128)S(1)} %get-tuple-element.190), channel_id=3, replica_groups=mesh['ta'=16,'sa'=8] {'ta','sa'}, use_global_device_ids=true, to_apply=%region_14.15.clone | all-reduce | flops 6144 | bytes 49152
  1039.8 343.3 %reduce-scatter.3.cloned.1.call-done = f32[24,2,128]{2,0,1:T(8,128)} async-done(((f32[24,256,128]{2,0,1:T(8,128)}), f32[24,2,128]{2,0,1:T(8,128)}) %reduce-scatter.3.cloned.1.call-update) | async-done | bytes 24592 | tf_op jit(solution)/shard_map/reduce_scatter | solution.py:122
  (481 shorter events, 440.9 us)
Async XLA Ops:
  7.2 17.5 %copy-start = (bf16[1,1,256,6144]{3,2,1,0:T(8,128)(2,1)S(1)}, bf16[1,1,256,6144]{3,2,1,0:T(8,128)(2,1)}, u32[]{:S(2)}) copy-start(bf16[1,1,256,6144]{3,2,1,0:T(8,128)(2,1)} %param.12) | copy-start | bytes 9437188
  7.2 396.2 %all-gather.3.cloned.1.call-start = ((), (), s32[]{:S(2)}) async-start(), calls=%async_computation.2 | async-start | bytes 4755456 | tf_op jit(solution)/shard_map/all_gather | solution.py:87
  7.2 20.8 %collective-permute-start = (bf16[256,6144]{1,0:T(8,128)(2,1)}, bf16[256,6144]{1,0:T(8,128)(2,1)}, u32[]{:S(2)}, u32[]{:S(2)}) collective-permute-start(bf16[256,6144]{1,0:T(8,128)(2,1)} %bitcast.93), channel_id=1, source_target_pairs={{0,8},{8,16},{16,24},{24,32},{32,40},{40,48},{48,56},{56,64},{64,7... | collective-permute-start | bytes 9437192 | tf_op jit(solution)/shard_map/ppermute | solution.py:14
  10.5 21.4 %collective-permute-start.1 = (bf16[256,6144]{1,0:T(8,128)(2,1)}, bf16[256,6144]{1,0:T(8,128)(2,1)}, u32[]{:S(2)}, u32[]{:S(2)}) collective-permute-start(bf16[256,6144]{1,0:T(8,128)(2,1)} %bitcast.94), channel_id=1, source_target_pairs={{8,0},{16,8},{24,16},{32,24},{40,32},{48,40},{56,48},{64,56},{72,6... | collective-permute-start | bytes 9437192 | tf_op jit(solution)/shard_map/ppermute | solution.py:14
  11.8 73.3 %collective-permute-start.2 = (bf16[256,6144]{1,0:T(8,128)(2,1)}, bf16[256,6144]{1,0:T(8,128)(2,1)}, u32[]{:S(2)}, u32[]{:S(2)}) collective-permute-start(bf16[256,6144]{1,0:T(8,128)(2,1)} %bitcast.95), channel_id=1, source_target_pairs={{0,1},{1,2},{2,3},{3,4},{4,5},{5,6},{6,7},{8,9},{9,10},{10,11},{11... | collective-permute-start | bytes 9437192 | tf_op jit(solution)/shard_map/ppermute | solution.py:14
  17.4 74.0 %collective-permute-start.3 = (bf16[256,6144]{1,0:T(8,128)(2,1)}, bf16[256,6144]{1,0:T(8,128)(2,1)}, u32[]{:S(2)}, u32[]{:S(2)}) collective-permute-start(bf16[256,6144]{1,0:T(8,128)(2,1)} %bitcast.96), channel_id=1, source_target_pairs={{1,0},{2,1},{3,2},{4,3},{5,4},{6,5},{7,6},{9,8},{10,9},{11,10},{12... | collective-permute-start | bytes 9437192 | tf_op jit(solution)/shard_map/ppermute | solution.py:14
  18.8 1364.3 %reduce-scatter.3.cloned.1.call-start = ((), (), s32[]{:S(2)}) async-start(), calls=%async_computation.1 | async-start | bytes 3170304 | tf_op jit(solution)/shard_map/reduce_scatter | solution.py:122
  753.2 123.6 %copy-start.2 = (f32[24,2]{1,0:T(8,128)S(1)}, f32[24,2]{1,0:T(8,128)}, u32[]{:S(2)}) copy-start(f32[24,2]{1,0:T(8,128)} %custom-call.10) | copy-start | bytes 580
  753.2 123.6 %copy-start.3 = (f32[24,2]{1,0:T(8,128)S(1)}, f32[24,2]{1,0:T(8,128)}, u32[]{:S(2)}) copy-start(f32[24,2]{1,0:T(8,128)} %custom-call.9) | copy-start | bytes 580
  970.9 412.2 %copy-start.1 = (f32[24,2,128]{2,0,1:T(8,128)S(1)}, f32[24,2,128]{2,0,1:T(8,128)}, u32[]{:S(2)}) copy-start(f32[24,2,128]{2,0,1:T(8,128)} %get-tuple-element.136) | copy-start | bytes 73732
Sparse Core Ops, SparseCore 0:
  18.9 384.4 all-gather.2
  742.5 640.5 reduce-scatter.2
where the time goes:
time: 1400 us; the launch traced here: 1390 us
  waiting for transfers between devices  665 us (48%)
  local copies, waits for them, and re-layouts  322 us (23%)
  matrix products  161 us (12%)
  blocking collectives  128 us (9%)
  loops' own time  48.5 us (3%)
  other arithmetic  41.1 us (3%)
  between operations  14.2 us (1%)
    reduce_scatter x1, waiting for transfers between devices, local(): lax.psum_scatter(mixes * factor[..., None], ('ta', 'sa'), scatter_dimensi...  343 us
    all_gather x1, waiting for transfers between devices, local(): gathered = lax.all_gather(text_qkv, ('ta', 'sa'), axis=0, tiled=True)  270 us
    dynamic_update_slice x24, local copies, waits for them, and re-layouts, attend(): stacked = lax.map(attend_one_head, jnp.arange(head_count, dtype=jnp.int32))  112 us
    dynamic_update_slice x120, local copies, waits for them, and re-layouts, partial_softmax(): return lax.map(partial_one_head, jnp.arange(head_count, dtype=jnp.int32))  95.7 us
    unnamed x1, blocking collectives  64.5 us
    pmax x1, blocking collectives, local(): global_peak = lax.pmax(tops, ('ta', 'sa'))  63.6 us
    ppermute x4, waiting for transfers between devices, from_behind(): return lax.ppermute(block, axis, route)  51.7 us
    dot_general x24, matrix products, attend_one_head(): jnp.dot(weights.astype(jnp.bfloat16), v_part, preferred_element_type=jnp....  48.4 us
  transfers between devices with their start and end apart: 6, of which 4 were waited for; matrix products, arithmetic and copies ran while one was open for 19% of the time, Pallas kernels for 0%

commit v1 on v0

v1 whole, which is shorter than its diff:
```python
import functools
import math

import jax
import jax.numpy as jnp
from jax import lax
from jax.experimental import pallas as pl
from jax.experimental.pallas import tpu as pltpu
from jax.sharding import PartitionSpec as P

HEAD = 128
D = 3072
TILE = 256
HEADS = 24
HALF = 12
CHUNKS = 12
CW = D // CHUNKS
TCOLS = 3 * D
THALF = TCOLS // 2
TQ = THALF // 2
SEC = TQ // 3
MESH = pl.DeviceIdType.MESH
C2 = math.log2(math.e) / math.sqrt(HEAD)
NEG = -1e30
PAIR, FAR, LEFT, RIGHT, OWN = 0, 1, 2, 3, 4


def qk(q, k):
    return lax.dot_general(q, k, (((1,), (1,)), ((), ())), preferred_element_type=jnp.float32)


def pv(p, v):
    return jnp.dot(p.astype(jnp.bfloat16), v, preferred_element_type=jnp.float32)


def merge(parts, stats, out, out_stats, last):
    top = functools.reduce(jnp.maximum, [m for m, _ in stats])
    weights = [jnp.exp2(m - top) for m, _ in stats]
    total = sum(w * l for w, (_, l) in zip(weights, stats))
    if last:
        weights = [w / total for w in weights]
    else:
        out_stats(top, total)
    for h in range(HALF):
        mixed = sum(
            w[..., h : h + 1] * part(h).astype(jnp.float32) for w, part in zip(weights, parts)
        )
        out(h, mixed.astype(jnp.bfloat16))


def kernel(
    q_hbm, kv_hbm, text_ref, mask_ref, pat_ref, video_ref, tout_ref,
    buf, q, stage, G, T, bias_ref, bias2_ref, Pt, PS, RB1, RS1, P2, S2, RB2, RS2, P3, S3, RB3, RS3, full,
    lsem, g_s, g_r, a_s, a_r, x_s, x_r, pair_s, pair_r, hs, hr, fwd_s, r_s, r_r,
):
    t = lax.axis_index("ta")
    s = lax.axis_index("sa")
    core = lax.rem(t, 2)
    y = lax.rem(t // 2, 4)
    x = lax.rem(s, 4)
    z = (t // 8) * 2 + s // 4
    g = x * 2 + core

    def dev(x_, y_, z_, core_):
        return ((z_ // 2) * 8 + y_ * 2 + core_, lax.rem(z_, 2) * 4 + x_)

    def up(v, i, n=4):
        return lax.rem(v + i, n)

    pair_t = t + 1 - 2 * core
    far_t = t + 2 * core - 1
    has_far = jnp.logical_and(far_t >= 0, far_t <= 15)
    has_left = s > 0
    has_right = s < 7
    far_cross = jnp.logical_or(t == 7, t == 8)
    far_relay = jnp.logical_or(t == 0, t == 15)
    relay_out_t = jnp.where(core == 1, 15, 0)
    relay_fin_t = jnp.where(t == 15, 8, 7)

    def g_peer(i):
        gg = up(g, i, 8)
        return dev(gg // 2, y, z, lax.rem(gg, 2))

    own_copy = pltpu.make_async_copy(kv_hbm, buf.at[OWN], lsem.at[0])
    q_copy = pltpu.make_async_copy(q_hbm, q, lsem.at[1])
    own_copy.start()
    q_copy.start()
    barrier = pltpu.get_barrier_semaphore()

    def greet(device):
        pl.semaphore_signal(barrier, inc=1, device_id=device, device_id_type=MESH)

    for i in range(1, 8):
        greet(g_peer(i))
    for i in range(1, 4):
        greet(dev(x, y, up(z, i), core))
        greet(dev(x, up(y, i), z, core))
    extra = [
        (has_far, (far_t, s)),
        (s == 3, (t, 4)),
        (s == 4, (t, 3)),
        (t == 15, (8, s)),
        (t == 8, (15, s)),
        (t == 0, (7, s)),
        (t == 7, (0, s)),
    ]
    for cond, device in extra:

        @pl.when(cond)
        def _():
            greet(device)

    rows = text_ref[...].astype(jnp.float32)
    w8 = TCOLS // 8
    stage[...] = jnp.concatenate(
        [rows[:, j * w8 : (j + 1) * w8] for j in range(8)], axis=0
    ).astype(jnp.bfloat16)

    pl.semaphore_wait(barrier, 13 + sum(jnp.where(cond, 1, 0) for cond, _ in extra))

    def remote(src, dst, ssem, rsem, device):
        return pltpu.make_async_remote_copy(
            src_ref=src, dst_ref=dst, send_sem=ssem, recv_sem=rsem,
            device_id=device, device_id_type=MESH,
        )

    def g_copy(i, slot):
        return remote(stage, G.at[slot], g_s.at[i], g_r.at[i], g_peer(i))

    for i in range(1, 8):
        g_copy(i, g).start()
    G[pl.ds(g, 1)] = stage[...][None]

    def cols(c, sec):
        return pl.ds(pl.multiple_of(c * CW + sec * D, 128), CW)

    def halo(k, c, sec, src, slot, device):
        return remote(
            src.at[:, cols(c, sec)], buf.at[slot, :, cols(c, sec)],
            hs.at[k], hr.at[slot, c, sec], device,
        )

    def send_halo(k, c):
        odd = lax.rem(c, 2) == 1
        if k == FAR:
            relay = jnp.logical_and(far_cross, odd)
            device = (jnp.where(relay, relay_out_t, far_t), s)
            slot = FAR
        elif k == LEFT:
            relay = jnp.logical_and(s == 4, odd)
            device = (t, jnp.where(relay, 0, s - 1))
            slot = jnp.where(relay, LEFT, RIGHT)
        else:
            relay = jnp.logical_and(s == 3, odd)
            device = (t, jnp.where(relay, 7, s + 1))
            slot = jnp.where(relay, RIGHT, LEFT)
        for sec in range(2):
            halo(k, c, sec, kv_hbm, slot, device).start()

    def send_loop(conds):
        @functools.partial(lax.fori_loop, 0, CHUNKS, init_val=0)
        def _(c, carry):
            for k, cond in conds:

                @pl.when(cond)
                def _():
                    send_halo(k, c)

            return carry

    send_loop([(LEFT, jnp.logical_and(has_left, s != 4)), (RIGHT, jnp.logical_and(has_right, s != 3))])

    def pair_copy():
        return remote(kv_hbm, buf.at[PAIR], pair_s, pair_r, (pair_t, s))

    pair_copy().start()

    for i in range(1, 8):
        g_copy(i, up(g, 8 - i, 8)).wait_recv()
    r_ = lax.broadcasted_iota(jnp.int32, (128, 128), 0)
    c_ = lax.broadcasted_iota(jnp.int32, (128, 128), 1)
    swap = (r_ // 16 == lax.rem(c_, 16) // 2) & (lax.rem(r_, 16) // 2 == c_ // 16)
    swap = swap & (lax.rem(r_, 2) == lax.rem(c_, 2))
    mixed_rows = jnp.dot(
        jnp.where(swap, 1.0, 0.0).astype(jnp.bfloat16),
        G[...].reshape(128, w8),
        preferred_element_type=jnp.float32,
    ).astype(jnp.bfloat16)
    def place(cc):
        for sec in range(3):
            for n in range(4):
                p = (sec * 4 + cc * 2) * 2 + n
                j, off = p // 3, (p % 3) * 384
                col = cc * THALF + (n // 2) * TQ + sec * SEC + (n % 2) * 384
                T[pl.ds(y, 1), pl.ds(z, 1), :, col : col + 384] = mixed_rows[
                    16 * j : 16 * j + 16, off : off + 384
                ][None, None]

    pl.when(core == 0)(lambda: place(0))
    pl.when(core == 1)(lambda: place(1))

    base = core * THALF
    ca = pl.ds(pl.multiple_of(base, 128), TQ)
    cb = pl.ds(pl.multiple_of(base + TQ, 128), TQ)

    def step_copy(step, half, i, yy, zz):
        along_z = (step == 0) == (half == 0)
        cs = ca if half == 0 else cb
        if step == 0:
            ref = T.at[yy, zz, :, cs]
        elif half == 0:
            ref = T.at[yy, :, :, cs]
        else:
            ref = T.at[:, zz, :, cs]
        device = dev(x, y, up(z, i), core) if along_z else dev(x, up(y, i), z, core)
        return remote(ref, ref, a_s.at[step, half, i], a_r.at[step, half, i], device)

    def step_waits(step):
        for half in range(2):
            along_z = (step == 0) == (half == 0)
            for i in range(1, 4):
                if along_z:
                    step_copy(step, half, i, y, up(z, 4 - i)).wait_recv()
                else:
                    step_copy(step, half, i, up(y, 4 - i), z).wait_recv()

    for step in range(2):
        for i in range(1, 4):
            for half in range(2):
                step_copy(step, half, i, y, z).start()
        step_waits(step)

    own_half = T.at[:, :, :, pl.ds(pl.multiple_of(base, 128), THALF)]
    other_half = T.at[:, :, :, pl.ds(pl.multiple_of(THALF - base, 128), THALF)]
    half_out = remote(own_half, own_half, x_s, x_r, (pair_t, s))
    half_in = remote(other_half, other_half, x_s, x_r, (pair_t, s))
    half_out.start()
    send_loop([(LEFT, s == 4), (RIGHT, s == 3)])

    r_ = lax.broadcasted_iota(jnp.int32, (256, 256), 0)
    c_ = lax.broadcasted_iota(jnp.int32, (256, 256), 1)
    by, bz, bx = c_ // 64, lax.rem(c_ // 16, 4), lax.rem(c_, 16) // 4
    bc, bi = lax.rem(c_ // 2, 2), lax.rem(c_, 2)
    row_of = (((bz // 2) * 8 + by * 2 + bc) * 8 + lax.rem(bz, 2) * 4 + bx) * 2 + bi
    valid = jnp.where(mask_ref[...] == 1, 1.0, 0.0)
    hot = jnp.where(r_ == row_of, 1.0, 0.0).astype(jnp.bfloat16)
    kept = jnp.dot(
        jnp.broadcast_to(valid, (8, 256)).astype(jnp.bfloat16), hot,
        preferred_element_type=jnp.float32,
    )
    bias = jnp.where(kept > 0.5, 0.0, NEG)
    bias_ref[...] = bias
    lane = lax.broadcasted_iota(jnp.int32, (8, 256), 1)
    mine = jnp.where(lane // 16 == y * 4 + z, 1, 0) * jnp.where(x == 0, 1, 0)
    bias2_ref[...] = jnp.where(mine == 1, bias, NEG)

    own_copy.wait()
    q_copy.wait()
    pair_copy().wait_recv()
    PS[...] = jnp.zeros_like(PS)

    def hcol(v):
        return pl.ds(pl.multiple_of(v, 128), HEAD)

    def text_cols(col):
        return T[:, :, :, hcol(col)].reshape(256, HEAD)

    @functools.partial(lax.fori_loop, 0, HALF, init_val=0)
    def _(hh, carry):
        col = base + (hh // 6) * TQ + lax.rem(hh, 6) * HEAD
        kcol = core * (D // 2) + hh * HEAD
        qx = text_cols(col)
        parts = [
            (qk(qx, buf[OWN, :, hcol(kcol)]), buf[OWN, :, hcol(kcol + D)]),
            (qk(qx, buf[PAIR, :, hcol(kcol)]), buf[PAIR, :, hcol(kcol + D)]),
            (qk(qx, text_cols(col + SEC)) + bias2_ref[0:1, :], text_cols(col + 2 * SEC)),
        ]
        top = functools.reduce(
            jnp.maximum, [jnp.max(sc, axis=1, keepdims=True) for sc, _ in parts]
        ) * C2
        ws = [jnp.exp2(sc * C2 - top) for sc, _ in parts]
        total = sum(jnp.sum(w, axis=1, keepdims=True) for w in ws)
        mixed = sum(pv(w, v) for w, (_, v) in zip(ws, parts))
        Pt[:, :, :, hcol(hh * HEAD)] = mixed.astype(jnp.bfloat16).reshape(4, 4, 16, HEAD)
        here = lax.broadcasted_iota(jnp.int32, (256, HEAD), 1) == hh
        for n, v in ((0, top), (1, total)):
            old = PS[n].reshape(256, HEAD)
            PS[n] = jnp.where(here, v, old).reshape(4, 4, 16, HEAD)
        return carry

    def r1(i, yy):
        device = dev(x, up(y, i), z, core)
        return (
            remote(Pt.at[yy], RB1.at[i - 1], r_s.at[0, i], r_r.at[0, i], device),
            remote(PS.at[:, yy], RS1.at[i - 1], r_s.at[1, i], r_r.at[1, i], device),
        )

    def r2(i, zz):
        device = dev(x, y, up(z, i), core)
        return (
            remote(P2.at[zz], RB2.at[i - 1], r_s.at[2, i], r_r.at[2, i], device),
            remote(S2.at[:, zz], RS2.at[i - 1], r_s.at[3, i], r_r.at[3, i], device),
        )

    def r3(i):
        device = dev(up(x, i), y, z, core)
        return (
            remote(P3, RB3.at[i - 1], r_s.at[4, i], r_r.at[4, i], device),
            remote(S3, RS3.at[i - 1], r_s.at[5, i], r_r.at[5, i], device),
        )

    for i in range(1, 4):
        for cp in r1(i, up(y, i)):
            cp.start()
    send_loop([(FAR, has_far)])

    def merge1():
        for i in range(1, 4):
            for cp in r1(i, up(y, i)):
                cp.wait_recv()
        stats = [(PS[0, y].reshape(64, HEAD), PS[1, y].reshape(64, HEAD))]
        stats += [(RS1[i, 0].reshape(64, HEAD), RS1[i, 1].reshape(64, HEAD)) for i in range(3)]

        def own(h):
            return Pt[y, :, :, h * HEAD : (h + 1) * HEAD].reshape(64, HEAD)

        def got(i):
            return lambda h: RB1[i, :, :, h * HEAD : (h + 1) * HEAD].reshape(64, HEAD)

        def out(h, v):
            P2[:, :, h * HEAD : (h + 1) * HEAD] = v.reshape(4, 16, HEAD)

        def out_stats(m, l):
            S2[0] = m.reshape(4, 16, HEAD)
            S2[1] = l.reshape(4, 16, HEAD)

        merge([own] + [got(i) for i in range(3)], stats, out, out_stats, False)
        for i in range(1, 4):
            for cp in r2(i, up(z, i)):
                cp.start()

    def merge2():
        for i in range(1, 4):
            for cp in r2(i, up(z, i)):
                cp.wait_recv()
        stats = [(S2[0, z], S2[1, z])] + [(RS2[i, 0], RS2[i, 1]) for i in range(3)]

        def own(h):
            return P2[z, :, h * HEAD : (h + 1) * HEAD]

        def got(i):
            return lambda h: RB2[i, :, h * HEAD : (h + 1) * HEAD]

        def out(h, v):
            P3[:, h * HEAD : (h + 1) * HEAD] = v

        def out_stats(m, l):
            S3[0] = m
            S3[1] = l

        merge([own] + [got(i) for i in range(3)], stats, out, out_stats, False)
        for i in range(1, 4):
            for cp in r3(i):
                cp.start()

    fcols = pl.ds(pl.multiple_of(core * (D // 2), 128), D // 2)
    ocols = pl.ds(pl.multiple_of((1 - core) * (D // 2), 128), D // 2)
    f_out = remote(full.at[:, fcols], full.at[:, fcols], r_s.at[6, 0], r_r.at[6, 0], (pair_t, s))
    f_in = remote(full.at[:, ocols], full.at[:, ocols], r_s.at[6, 0], r_r.at[6, 0], (pair_t, s))

    def merge3():
        for i in range(1, 4):
            for cp in r3(i):
                cp.wait_recv()
        stats = [(S3[0], S3[1])] + [(RS3[i, 0], RS3[i, 1]) for i in range(3)]

        def own(h):
            return P3[:, h * HEAD : (h + 1) * HEAD]

        def got(i):
            return lambda h: RB3[i, :, h * HEAD : (h + 1) * HEAD]

        def out(h, v):
            full[:, hcol(core * (D // 2) + h * HEAD)] = v

        merge([own] + [got(i) for i in range(3)], stats, out, None, True)
        f_out.start()

    half_in.wait_recv()
    number = [(pair_t, s), (far_t, s), (t, s - 1), (t, s + 1)]
    exists = [None, has_far, has_left, has_right]
    seen = []
    for k in range(4):
        tile = number[k][0] * 8 + number[k][1]
        hit = jnp.int32(0)
        for n in range(4):
            hit = hit + jnp.where(pat_ref[n] == tile, 1, 0)
        if exists[k] is not None:
            hit = hit * jnp.where(exists[k], 1, 0)
        seen.append(hit)
    slots = [PAIR] + [jnp.where(exists[k], k, OWN) for k in (FAR, LEFT, RIGHT)]
    drop = [jnp.where(h > 0, 0.0, NEG).astype(jnp.float32) for h in seen]

    def relay(c):
        def forward(cond, k_sem, slot, to_slot, device):
            @pl.when(cond)
            def _():
                for sec in range(2):
                    halo(0, c, sec, kv_hbm, slot, device).wait_recv()
                    remote(
                        buf.at[slot, :, cols(c, sec)], buf.at[to_slot, :, cols(c, sec)],
                        fwd_s.at[k_sem], hr.at[to_slot, c, sec], device,
                    ).start()

        forward(s == 7, 0, RIGHT, LEFT, (t, 4))
        forward(s == 0, 0, LEFT, RIGHT, (t, 3))
        forward(far_relay, 1, FAR, FAR, (relay_fin_t, s))

    def video(c):
        for k in (FAR, LEFT, RIGHT):

            @pl.when(exists[k])
            def _():
                for sec in range(2):
                    halo(0, c, sec, kv_hbm, k, (t, s)).wait_recv()

        for hh in range(2):
            col = c * CW + hh * HEAD
            tcol = (c // 3) * TQ + lax.rem(c, 3) * CW + hh * HEAD
            qh = q[:, hcol(col)]
            sc = [qk(qh, buf[OWN, :, hcol(col)])]
            sc += [qk(qh, buf[slots[k], :, hcol(col)]) for k in range(4)]
            sc.append(qk(qh, text_cols(tcol + SEC)) + bias_ref[0:1, :])
            tops = [jnp.max(v, axis=1, keepdims=True) for v in sc]
            for k in range(4):
                tops[1 + k] = tops[1 + k] + drop[k]
            top = functools.reduce(jnp.maximum, tops) * C2
            lows = [top] + [top - drop[k] for k in range(4)] + [top]
            ws = [jnp.exp2(v * C2 - low) for v, low in zip(sc, lows)]
            total = sum(jnp.sum(w, axis=1, keepdims=True) for w in ws)
            vs = [buf[OWN, :, hcol(col + D)]]
            vs += [buf[slots[k], :, hcol(col + D)] for k in range(4)]
            vs.append(text_cols(tcol + 2 * SEC))
            mixed = sum(pv(w, v) for w, v in zip(ws, vs))
            video_ref[:, hcol(col)] = (mixed / total).astype(jnp.bfloat16)

    @functools.partial(lax.fori_loop, 0, CHUNKS, init_val=0)
    def _(c, carry):
        @pl.when(lax.rem(c, 2) == 0)
        def _():
            relay(c + 1)

        pl.when(c == 6)(merge1)
        pl.when(c == 9)(merge2)
        video(c)
        return carry

    merge3()
    f_in.wait_recv()
    pick_r = lax.broadcasted_iota(jnp.int32, (16, 16), 0)
    pick_c = lax.broadcasted_iota(jnp.int32, (16, 16), 1)
    pick = jnp.where(pick_c == pick_r + 2 * g, 1.0, 0.0).astype(jnp.bfloat16)
    chosen = jnp.dot(pick, full[...], preferred_element_type=jnp.float32)
    tout_ref[...] = chosen[:2].astype(jnp.bfloat16)

    for i in range(1, 8):
        g_copy(i, g).wait_send()
    for step in range(2):
        for i in range(1, 4):
            for half in range(2):
                step_copy(step, half, i, y, z).wait_send()
    half_out.wait_send()
    pair_copy().wait_send()

    def drain(cond, sem, width):
        @pl.when(cond)
        def _():
            ref = buf.at[OWN, :, pl.ds(0, width)]
            remote(ref, ref, sem, hr.at[0, 0, 0], (pair_t, s)).wait_send()

    drain(has_far, hs.at[FAR], 2 * D)
    drain(has_left, hs.at[LEFT], 2 * D)
    drain(has_right, hs.at[RIGHT], 2 * D)
    drain(jnp.logical_or(s == 0, s == 7), fwd_s.at[0], D)
    drain(far_relay, fwd_s.at[1], D)
    for i in range(1, 4):
        for cp in r1(i, up(y, i)) + r2(i, up(z, i)) + r3(i):
            cp.wait_send()
    f_out.wait_send()


def local(video_q, video_kv, text_qkv, text_mask, pattern):
    bf, f32 = jnp.bfloat16, jnp.float32
    dma = pltpu.SemaphoreType.DMA
    vm = pltpu.VMEM
    whole = pl.BlockSpec(memory_space=pltpu.VMEM)
    hbm = pl.BlockSpec(memory_space=pl.ANY)
    scratch = [
        vm((5, TILE, 2 * D), bf),
        vm((TILE, D), bf),
        vm((16, TCOLS // 8), bf),
        vm((8, 16, TCOLS // 8), bf),
        vm((4, 4, 16, TCOLS), bf),
        vm((8, 256), f32),
        vm((8, 256), f32),
        vm((4, 4, 16, D // 2), bf),
        vm((2, 4, 4, 16, HEAD), f32),
        vm((3, 4, 16, D // 2), bf),
        vm((3, 2, 4, 16, HEAD), f32),
        vm((4, 16, D // 2), bf),
        vm((2, 4, 16, HEAD), f32),
        vm((3, 16, D // 2), bf),
        vm((3, 2, 16, HEAD), f32),
        vm((16, D // 2), bf),
        vm((2, 16, HEAD), f32),
        vm((3, 16, D // 2), bf),
        vm((3, 2, 16, HEAD), f32),
        vm((16, D), bf),
        dma((2,)), dma((8,)), dma((8,)), dma((2, 2, 4)), dma((2, 2, 4)),
        dma, dma, dma, dma, dma((4,)), dma((4, CHUNKS, 2)), dma((2,)), dma((7, 4)), dma((7, 4)),
    ]
    video_out, text_out = pl.pallas_call(
        kernel,
        out_shape=(jax.ShapeDtypeStruct((TILE, D), bf), jax.ShapeDtypeStruct((2, D), bf)),
        in_specs=[hbm, hbm, whole, whole, pl.BlockSpec(memory_space=pltpu.SMEM)],
        out_specs=(whole, whole),
        scratch_shapes=scratch,
        compiler_params=pltpu.CompilerParams(
            collective_id=0, has_side_effects=True, vmem_limit_bytes=58 * 2**20
        ),
        cost_estimate=pl.CostEstimate(
            flops=6 * 10**9, bytes_accessed=10**7, transcendentals=12 * 10**6
        ),
    )(video_q[0, 0], video_kv[0, 0], text_qkv, text_mask.reshape(1, 256), pattern.reshape(4))
    return video_out[None, None], text_out


def solution(mesh):
    in_specs = (
        P("ta", "sa", None, None),
        P("ta", "sa", None, None),
        P(("ta", "sa"), None),
        P(),
        P("ta", "sa", None),
    )
    out_specs = (P("ta", "sa", None, None), P(("ta", "sa"), None))
    return jax.shard_map(local, mesh=mesh, in_specs=in_specs, out_specs=out_specs, check_vma=False)
```

time: 1400 us -> 116 us (0.08)
  the two profiles are of different devices: /device:TPU:0 before, /device:TPU:31 now
where the time goes in v1:
time: 116 us; the launch traced here: 114 us
  Pallas kernels  110 us (95%)
  local copies, waits for them, and re-layouts  3.26 us (3%)
    pallas_call x1, Pallas kernels, local(): pl.pallas_call(kernel, out_shape=(jax.ShapeDtypeStruct((TILE, D), bf), ja...  110 us
    unnamed x4, local copies, waits for them, and re-layouts  3.26 us

profile of v1, /device:TPU:31, one launch (start us, length us, event | category | flops | bytes accessed | tf_op | source)
XLA Modules:
  0.0 114.1 jit_solution(15199147748069456557)
XLA Ops:
  0.6 110.1 %shard_map.68 = (bf16[256,3072]{1,0:T(8,128)(2,1)}, bf16[2,3072]{1,0:T(2,128)(2,1)}) custom-call(bf16[256,3072]{1,0:T(8,128)(2,1)} %bitcast.7, bf16[256,6144]{1,0:T(8,128)(2,1)} %bitcast.6, bf16[2,9216]{1,0:T(2,128)(2,1)} %text_ref.1, s32[1,256]{1,0:T(1,128)} %bitcast.8, s32[4]{0:T(128)} %bitcast.9), custom_call_target="tpu_custom_call" | custom-call | flops 6000000000 | bytes 10000000 | tf_op jit(solution)/shard_map/pallas_call | solution.py:522
  110.8 0.0 copy-start
  110.8 2.7 %copy.9 = bf16[1,1,256,3072]{3,2,1,0:T(8,128)(2,1)} copy(bf16[1,1,256,3072]{3,2,1,0:T(8,128)(2,1)} %bitcast.5) | data formatting | bytes 3145728
  113.5 0.0 copy-done
  113.5 0.6 copy.10
Async XLA Ops:
  110.8 2.7 %copy-start = (bf16[2,3072]{1,0:T(2,128)(2,1)S(1)}, bf16[2,3072]{1,0:T(2,128)(2,1)}, u32[]{:S(2)}) copy-start(bf16[2,3072]{1,0:T(2,128)(2,1)} %get-tuple-element.9) | copy-start | bytes 36868

commit v2 on v1

--- a/solution.py
+++ b/solution.py
@@ -22,6 +22,7 @@
 MESH = pl.DeviceIdType.MESH
 C2 = math.log2(math.e) / math.sqrt(HEAD)
 NEG = -1e30
+FAR_EARLY, X_EARLY, AT1, AT2 = 3, 10, 1, 5
 PAIR, FAR, LEFT, RIGHT, OWN = 0, 1, 2, 3, 4
 
 
@@ -50,8 +51,8 @@
 
 def kernel(
     q_hbm, kv_hbm, text_ref, mask_ref, pat_ref, video_ref, tout_ref,
-    buf, q, stage, G, T, bias_ref, bias2_ref, Pt, PS, RB1, RS1, P2, S2, RB2, RS2, P3, S3, RB3, RS3, full,
-    lsem, g_s, g_r, a_s, a_r, x_s, x_r, pair_s, pair_r, hs, hr, fwd_s, r_s, r_r,
+    buf, q, stage, G, T, bias_ref, bias2_ref, Pt, PS, RB1, RS1, P2, S2, RB2, RS2, P3, S3, RB3, RS3, TT, ST, full,
+    lsem, g_s, g_r, a_s, a_r, b_s, b_r, x_s, x_r, pair_s, pair_r, hs, hr, fwd_s, r_s, r_r,
 ):
     t = lax.axis_index("ta")
     s = lax.axis_index("sa")
@@ -74,8 +75,6 @@
     has_right = s < 7
     far_cross = jnp.logical_or(t == 7, t == 8)
     far_relay = jnp.logical_or(t == 0, t == 15)
-    relay_out_t = jnp.where(core == 1, 15, 0)
-    relay_fin_t = jnp.where(t == 15, 8, 7)
 
     def g_peer(i):
         gg = up(g, i, 8)
@@ -97,8 +96,6 @@
         greet(dev(x, up(y, i), z, core))
     extra = [
         (has_far, (far_t, s)),
-        (s == 3, (t, 4)),
-        (s == 4, (t, 3)),
         (t == 15, (8, s)),
         (t == 8, (15, s)),
         (t == 0, (7, s)),
@@ -143,23 +140,22 @@
     def send_halo(k, c):
         odd = lax.rem(c, 2) == 1
         if k == FAR:
-            relay = jnp.logical_and(far_cross, odd)
-            device = (jnp.where(relay, relay_out_t, far_t), s)
+            out_t = jnp.where((t == 7) == odd, 15, 0)
+            device = (jnp.where(far_cross, out_t, far_t), s)
             slot = FAR
-        elif k == LEFT:
-            relay = jnp.logical_and(s == 4, odd)
-            device = (t, jnp.where(relay, 0, s - 1))
-            slot = jnp.where(relay, LEFT, RIGHT)
         else:
-            relay = jnp.logical_and(s == 3, odd)
-            device = (t, jnp.where(relay, 7, s + 1))
-            slot = jnp.where(relay, RIGHT, LEFT)
+            edge = 3 if k == RIGHT else 4
+            out_s = jnp.where((s == 3) == odd, 7, 0)
+            normal = s + 1 if k == RIGHT else s - 1
+            device = (t, jnp.where(s == edge, out_s, normal))
+            slot = jnp.where(s == edge, jnp.where(out_s == 7, RIGHT, LEFT), LEFT if k == RIGHT else RIGHT)
         for sec in range(2):
             halo(k, c, sec, kv_hbm, slot, device).start()
 
-    def send_loop(conds):
-        @functools.partial(lax.fori_loop, 0, CHUNKS, init_val=0)
-        def _(c, carry):
+    def send_loop(first, last, conds, stride=1):
+        @functools.partial(lax.fori_loop, 0, (last - first + stride - 1) // stride, init_val=0)
+        def _(n, carry):
+            c = first + n * stride
             for k, cond in conds:
 
                 @pl.when(cond)
@@ -168,12 +164,43 @@
 
             return carry
 
-    send_loop([(LEFT, jnp.logical_and(has_left, s != 4)), (RIGHT, jnp.logical_and(has_right, s != 3))])
+    along_x = [
+        (LEFT, jnp.logical_and(has_left, s != 4)),
+        (RIGHT, jnp.logical_and(has_right, s != 3)),
+    ]
+    crossing = [(LEFT, s == 4), (RIGHT, s == 3)]
+    send_loop(0, 1, along_x + crossing)
+    send_loop(0, FAR_EARLY, [(FAR, has_far)])
+    send_loop(1, 2, crossing)
+    send_loop(1, X_EARLY, along_x)
+    send_loop(2, CHUNKS, crossing, 2)
 
     def pair_copy():
         return remote(kv_hbm, buf.at[PAIR], pair_s, pair_r, (pair_t, s))
 
     pair_copy().start()
+
+    def forward(cond, c, sem, slot, to_slot, device):
+        @pl.when(cond)
+        def _():
+            for sec in range(2):
+                halo(0, c, sec, kv_hbm, slot, device).wait_recv()
+                remote(
+                    buf.at[slot, :, cols(c, sec)], buf.at[to_slot, :, cols(c, sec)],
+                    sem, hr.at[to_slot, c, sec], device,
+                ).start()
+
+    def relay_x(c, on=True):
+        odd = lax.rem(c, 2) == 1
+        to_s = jnp.where((s == 7) == odd, 4, 3)
+        edge = jnp.logical_and(jnp.logical_or(s == 0, s == 7), on)
+        slot = jnp.where(s == 7, RIGHT, LEFT)
+        forward(edge, c, fwd_s.at[0], slot, jnp.where(to_s == 4, LEFT, RIGHT), (t, to_s))
+
+    def relay_t(c, on=True):
+        odd = lax.rem(c, 2) == 1
+        to_t = jnp.where((t == 15) == odd, 8, 7)
+        forward(jnp.logical_and(far_relay, on), c, fwd_s.at[1], FAR, FAR, (to_t, s))
 
     for i in range(1, 8):
         g_copy(i, up(g, 8 - i, 8)).wait_recv()
@@ -200,12 +227,11 @@
     pl.when(core == 1)(lambda: place(1))
 
     base = core * THALF
-    ca = pl.ds(pl.multiple_of(base, 128), TQ)
-    cb = pl.ds(pl.multiple_of(base + TQ, 128), TQ)
-
-    def step_copy(step, half, i, yy, zz):
+
+    def step_copy(step, part, half, i, yy, zz):
         along_z = (step == 0) == (half == 0)
-        cs = ca if half == 0 else cb
+        width = (TQ, SEC, 2 * SEC)[part]
+        cs = pl.ds(pl.multiple_of(base + half * TQ + (SEC if part == 2 else 0), 128), width)
         if step == 0:
             ref = T.at[yy, zz, :, cs]
         elif half == 0:
@@ -213,29 +239,28 @@
         else:
             ref = T.at[:, zz, :, cs]
         device = dev(x, y, up(z, i), core) if along_z else dev(x, up(y, i), z, core)
-        return remote(ref, ref, a_s.at[step, half, i], a_r.at[step, half, i], device)
-
-    def step_waits(step):
+        return remote(ref, ref, a_s.at[part, half, i], a_r.at[part, half, i], device)
+
+    def step_starts(step, part):
+        for i in (2, 1, 3):
+            for half in range(2):
+                step_copy(step, part, half, i, y, z).start()
+
+    def step_waits(step, part):
         for half in range(2):
             along_z = (step == 0) == (half == 0)
             for i in range(1, 4):
                 if along_z:
-                    step_copy(step, half, i, y, up(z, 4 - i)).wait_recv()
+                    step_copy(step, part, half, i, y, up(z, 4 - i)).wait_recv()
                 else:
-                    step_copy(step, half, i, up(y, 4 - i), z).wait_recv()
-
-    for step in range(2):
-        for i in range(1, 4):
-            for half in range(2):
-                step_copy(step, half, i, y, z).start()
-        step_waits(step)
-
-    own_half = T.at[:, :, :, pl.ds(pl.multiple_of(base, 128), THALF)]
-    other_half = T.at[:, :, :, pl.ds(pl.multiple_of(THALF - base, 128), THALF)]
-    half_out = remote(own_half, own_half, x_s, x_r, (pair_t, s))
-    half_in = remote(other_half, other_half, x_s, x_r, (pair_t, s))
-    half_out.start()
-    send_loop([(LEFT, s == 4), (RIGHT, s == 3)])
+                    step_copy(step, part, half, i, up(y, 4 - i), z).wait_recv()
+
+    step_starts(0, 0)
+    step_waits(0, 0)
+    step_starts(1, 1)
+    step_starts(1, 2)
+    send_loop(3, 6, crossing, 2)
+    send_loop(3, CHUNKS, [(FAR, far_cross)], 2)
 
     r_ = lax.broadcasted_iota(jnp.int32, (256, 256), 0)
     c_ = lax.broadcasted_iota(jnp.int32, (256, 256), 1)
@@ -251,12 +276,16 @@
     bias = jnp.where(kept > 0.5, 0.0, NEG)
     bias_ref[...] = bias
     lane = lax.broadcasted_iota(jnp.int32, (8, 256), 1)
-    mine = jnp.where(lane // 16 == y * 4 + z, 1, 0) * jnp.where(x == 0, 1, 0)
-    bias2_ref[...] = jnp.where(mine == 1, bias, NEG)
+    bias2_ref[...] = jnp.where(lane // 64 == x, bias, NEG)
 
     own_copy.wait()
     q_copy.wait()
     pair_copy().wait_recv()
+    step_waits(1, 1)
+    for c in (0, 2, 4):
+        relay_x(c)
+    for c in (0, 2):
+        relay_t(c)
     PS[...] = jnp.zeros_like(PS)
 
     def hcol(v):
@@ -273,7 +302,6 @@
         parts = [
             (qk(qx, buf[OWN, :, hcol(kcol)]), buf[OWN, :, hcol(kcol + D)]),
             (qk(qx, buf[PAIR, :, hcol(kcol)]), buf[PAIR, :, hcol(kcol + D)]),
-            (qk(qx, text_cols(col + SEC)) + bias2_ref[0:1, :], text_cols(col + 2 * SEC)),
         ]
         top = functools.reduce(
             jnp.maximum, [jnp.max(sc, axis=1, keepdims=True) for sc, _ in parts]
@@ -312,7 +340,33 @@
     for i in range(1, 4):
         for cp in r1(i, up(y, i)):
             cp.start()
-    send_loop([(FAR, has_far)])
+    send_loop(FAR_EARLY, CHUNKS, [(FAR, jnp.logical_and(has_far, jnp.logical_not(far_cross)))])
+    send_loop(4, CHUNKS, [(FAR, far_cross)], 2)
+
+    step_waits(1, 2)
+
+    def half_copy(ab, which):
+        cs = pl.ds(pl.multiple_of(which * THALF + ab * TQ + SEC, 128), 2 * SEC)
+        ref = T.at[:, :, :, cs]
+        return remote(ref, ref, b_s.at[ab], b_r.at[ab], (pair_t, s))
+
+    for ab in range(2):
+        half_copy(ab, core).start()
+
+    ST[...] = jnp.zeros_like(ST)
+
+    @functools.partial(lax.fori_loop, 0, HALF, init_val=0)
+    def _(hh, carry):
+        col = base + (hh // 6) * TQ + lax.rem(hh, 6) * HEAD
+        sc = qk(T[y, z, :, hcol(col)], text_cols(col + SEC)) + bias2_ref[0:1, :]
+        top = jnp.max(sc, axis=1, keepdims=True) * C2
+        w = jnp.exp2(sc * C2 - top)
+        TT[:, hcol(hh * HEAD)] = pv(w, text_cols(col + 2 * SEC)).astype(jnp.bfloat16)
+        here = lax.broadcasted_iota(jnp.int32, (16, HEAD), 1) == hh
+        for n, v in ((0, top), (1, jnp.sum(w, axis=1, keepdims=True))):
+            ST[n] = jnp.where(here, v, ST[n])
+        return carry
+
 
     def merge1():
         for i in range(1, 4):
@@ -344,6 +398,10 @@
             for cp in r2(i, up(z, i)):
                 cp.wait_recv()
         stats = [(S2[0, z], S2[1, z])] + [(RS2[i, 0], RS2[i, 1]) for i in range(3)]
+        stats.append((ST[0], ST[1]))
+
+        def local_text(h):
+            return TT[:, h * HEAD : (h + 1) * HEAD]
 
         def own(h):
             return P2[z, :, h * HEAD : (h + 1) * HEAD]
@@ -358,10 +416,11 @@
             S3[0] = m
             S3[1] = l
 
-        merge([own] + [got(i) for i in range(3)], stats, out, out_stats, False)
+        merge([own] + [got(i) for i in range(3)] + [local_text], stats, out, out_stats, False)
         for i in range(1, 4):
             for cp in r3(i):
                 cp.start()
+        send_loop(X_EARLY, CHUNKS, along_x)
 
     fcols = pl.ds(pl.multiple_of(core * (D // 2), 128), D // 2)
     ocols = pl.ds(pl.multiple_of((1 - core) * (D // 2), 128), D // 2)
@@ -386,7 +445,8 @@
         merge([own] + [got(i) for i in range(3)], stats, out, None, True)
         f_out.start()
 
-    half_in.wait_recv()
+    for ab in range(2):
+        half_copy(ab, 1 - core).wait_recv()
     number = [(pair_t, s), (far_t, s), (t, s - 1), (t, s + 1)]
     exists = [None, has_far, has_left, has_right]
     seen = []
@@ -400,21 +460,6 @@
         seen.append(hit)
     slots = [PAIR] + [jnp.where(exists[k], k, OWN) for k in (FAR, LEFT, RIGHT)]
     drop = [jnp.where(h > 0, 0.0, NEG).astype(jnp.float32) for h in seen]
-
-    def relay(c):
-        def forward(cond, k_sem, slot, to_slot, device):
-            @pl.when(cond)
-            def _():
-                for sec in range(2):
-                    halo(0, c, sec, kv_hbm, slot, device).wait_recv()
-                    remote(
-                        buf.at[slot, :, cols(c, sec)], buf.at[to_slot, :, cols(c, sec)],
-                        fwd_s.at[k_sem], hr.at[to_slot, c, sec], device,
-                    ).start()
-
-        forward(s == 7, 0, RIGHT, LEFT, (t, 4))
-        forward(s == 0, 0, LEFT, RIGHT, (t, 3))
-        forward(far_relay, 1, FAR, FAR, (relay_fin_t, s))
 
     def video(c):
         for k in (FAR, LEFT, RIGHT):
@@ -444,18 +489,29 @@
             mixed = sum(pv(w, v) for w, v in zip(ws, vs))
             video_ref[:, hcol(col)] = (mixed / total).astype(jnp.bfloat16)
 
+    relay_x(1)
+    relay_t(1)
+
     @functools.partial(lax.fori_loop, 0, CHUNKS, init_val=0)
     def _(c, carry):
-        @pl.when(lax.rem(c, 2) == 0)
+        odd = lax.rem(c, 2)
+        relay_x(jnp.where(odd == 1, c + 2, c + 6), c < jnp.where(odd == 1, 10, 6))
+        relay_t(c + 3, c < CHUNKS - 3)
+
+        @pl.when(jnp.logical_and(odd == 0, c < 6))
         def _():
-            relay(c + 1)
-
-        pl.when(c == 6)(merge1)
-        pl.when(c == 9)(merge2)
+            for k, cond in crossing:
+
+                @pl.when(cond)
+                def _():
+                    send_halo(k, c + 7)
+
+        pl.when(c == AT1)(merge1)
+        pl.when(c == AT2)(merge2)
+        pl.when(c == CHUNKS - 1)(merge3)
         video(c)
         return carry
 
-    merge3()
     f_in.wait_recv()
     pick_r = lax.broadcasted_iota(jnp.int32, (16, 16), 0)
     pick_c = lax.broadcasted_iota(jnp.int32, (16, 16), 1)
@@ -465,11 +521,12 @@
 
     for i in range(1, 8):
         g_copy(i, g).wait_send()
-    for step in range(2):
+    for part in range(3):
         for i in range(1, 4):
             for half in range(2):
-                step_copy(step, half, i, y, z).wait_send()
-    half_out.wait_send()
+                step_copy(min(part, 1), part, half, i, y, z).wait_send()
+    for ab in range(2):
+        half_copy(ab, core).wait_send()
     pair_copy().wait_send()
 
     def drain(cond, sem, width):
@@ -481,8 +538,8 @@
     drain(has_far, hs.at[FAR], 2 * D)
     drain(has_left, hs.at[LEFT], 2 * D)
     drain(has_right, hs.at[RIGHT], 2 * D)
-    drain(jnp.logical_or(s == 0, s == 7), fwd_s.at[0], D)
-    drain(far_relay, fwd_s.at[1], D)
+    drain(jnp.logical_or(s == 0, s == 7), fwd_s.at[0], 2 * D)
+    drain(far_relay, fwd_s.at[1], 2 * D)
     for i in range(1, 4):
         for cp in r1(i, up(y, i)) + r2(i, up(z, i)) + r3(i):
             cp.wait_send()
@@ -515,9 +572,11 @@
         vm((2, 16, HEAD), f32),
         vm((3, 16, D // 2), bf),
         vm((3, 2, 16, HEAD), f32),
+        vm((16, D // 2), bf),
+        vm((2, 16, HEAD), f32),
         vm((16, D), bf),
-        dma((2,)), dma((8,)), dma((8,)), dma((2, 2, 4)), dma((2, 2, 4)),
-        dma, dma, dma, dma, dma((4,)), dma((4, CHUNKS, 2)), dma((2,)), dma((7, 4)), dma((7, 4)),
+        dma((2,)), dma((8,)), dma((8,)), dma((3, 2, 4)), dma((3, 2, 4)),
+        dma((2,)), dma((2,)), dma, dma, dma, dma, dma((4,)), dma((4, CHUNKS, 2)), dma((2,)), dma((7, 4)), dma((7, 4)),
     ]
     video_out, text_out = pl.pallas_call(
         kernel,

time: 116 us -> 103 us (0.89)
  the two profiles are of different devices: /device:TPU:31 before, /device:TPU:6 now
where the time goes in v2:
time: 103 us; the launch traced here: 102 us
  Pallas kernels  98.5 us (96%)
  local copies, waits for them, and re-layouts  3.26 us (3%)
    pallas_call x1, Pallas kernels, local(): pl.pallas_call(kernel, out_shape=(jax.ShapeDtypeStruct((TILE, D), bf), ja...  98.5 us
    unnamed x4, local copies, waits for them, and re-layouts  3.26 us

profile of v2, /device:TPU:6, one launch (start us, length us, event | category | flops | bytes accessed | tf_op | source)
XLA Modules:
  0.0 102.4 jit_solution(16338341178864693319)
XLA Ops:
  0.6 98.5 %shard_map.68 = (bf16[256,3072]{1,0:T(8,128)(2,1)}, bf16[2,3072]{1,0:T(2,128)(2,1)}) custom-call(bf16[256,3072]{1,0:T(8,128)(2,1)} %bitcast.7, bf16[256,6144]{1,0:T(8,128)(2,1)} %bitcast.6, bf16[2,9216]{1,0:T(2,128)(2,1)} %text_ref.1, s32[1,256]{1,0:T(1,128)} %bitcast.8, s32[4]{0:T(128)} %bitcast.9), custom_call_target="tpu_custom_call" | custom-call | flops 6000000000 | bytes 10000000 | tf_op jit(solution)/shard_map/pallas_call | solution.py:581
  99.2 0.0 copy-start
  99.2 2.7 %copy.9 = bf16[1,1,256,3072]{3,2,1,0:T(8,128)(2,1)} copy(bf16[1,1,256,3072]{3,2,1,0:T(8,128)(2,1)} %bitcast.5) | data formatting | bytes 3145728
  101.8 0.0 copy-done
  101.8 0.6 copy.10
Async XLA Ops:
  99.2 2.7 %copy-start = (bf16[2,3072]{1,0:T(2,128)(2,1)S(1)}, bf16[2,3072]{1,0:T(2,128)(2,1)}, u32[]{:S(2)}) copy-start(bf16[2,3072]{1,0:T(2,128)(2,1)} %get-tuple-element.9) | copy-start | bytes 36868

commit v3 on v2

--- a/solution.py
+++ b/solution.py
@@ -22,7 +22,7 @@
 MESH = pl.DeviceIdType.MESH
 C2 = math.log2(math.e) / math.sqrt(HEAD)
 NEG = -1e30
-FAR_EARLY, X_EARLY, AT1, AT2 = 3, 10, 1, 5
+FAR_EARLY, X_EARLY, AT1, AT2 = 3, 11, 1, 6
 PAIR, FAR, LEFT, RIGHT, OWN = 0, 1, 2, 3, 4
 
 
@@ -50,8 +50,8 @@
 
 
 def kernel(
-    q_hbm, kv_hbm, text_ref, mask_ref, pat_ref, video_ref, tout_ref,
-    buf, q, stage, G, T, bias_ref, bias2_ref, Pt, PS, RB1, RS1, P2, S2, RB2, RS2, P3, S3, RB3, RS3, TT, ST, full,
+    q_hbm, kv_hbm, text_hbm, mask_hbm, pat_ref, video_hbm, tout_ref,
+    text_ref, mask_ref, video_ref, buf, q, stage, G, T, bias_ref, bias2_ref, Pt, PS, RB1, RS1, P2, S2, RB2, RS2, P3, S3, RB3, RS3, TT, ST, full,
     lsem, g_s, g_r, a_s, a_r, b_s, b_r, x_s, x_r, pair_s, pair_r, hs, hr, fwd_s, r_s, r_r,
 ):
     t = lax.axis_index("ta")
@@ -82,8 +82,10 @@
 
     own_copy = pltpu.make_async_copy(kv_hbm, buf.at[OWN], lsem.at[0])
     q_copy = pltpu.make_async_copy(q_hbm, q, lsem.at[1])
-    own_copy.start()
-    q_copy.start()
+    text_copy = pltpu.make_async_copy(text_hbm, text_ref, lsem.at[2])
+    mask_copy = pltpu.make_async_copy(mask_hbm, mask_ref, lsem.at[3])
+    text_copy.start()
+    mask_copy.start()
     barrier = pltpu.get_barrier_semaphore()
 
     def greet(device):
@@ -107,6 +109,9 @@
         def _():
             greet(device)
 
+    own_copy.start()
+    q_copy.start()
+    text_copy.wait()
     rows = text_ref[...].astype(jnp.float32)
     w8 = TCOLS // 8
     stage[...] = jnp.concatenate(
@@ -256,6 +261,8 @@
                     step_copy(step, part, half, i, up(y, 4 - i), z).wait_recv()
 
     step_starts(0, 0)
+    relay_x(0)
+    relay_t(0)
     step_waits(0, 0)
     step_starts(1, 1)
     step_starts(1, 2)
@@ -267,6 +274,7 @@
     by, bz, bx = c_ // 64, lax.rem(c_ // 16, 4), lax.rem(c_, 16) // 4
     bc, bi = lax.rem(c_ // 2, 2), lax.rem(c_, 2)
     row_of = (((bz // 2) * 8 + by * 2 + bc) * 8 + lax.rem(bz, 2) * 4 + bx) * 2 + bi
+    mask_copy.wait()
     valid = jnp.where(mask_ref[...] == 1, 1.0, 0.0)
     hot = jnp.where(r_ == row_of, 1.0, 0.0).astype(jnp.bfloat16)
     kept = jnp.dot(
@@ -282,10 +290,9 @@
     q_copy.wait()
     pair_copy().wait_recv()
     step_waits(1, 1)
-    for c in (0, 2, 4):
+    for c in (2, 4):
         relay_x(c)
-    for c in (0, 2):
-        relay_t(c)
+    relay_t(2)
     PS[...] = jnp.zeros_like(PS)
 
     def hcol(v):
@@ -488,25 +495,28 @@
             vs.append(text_cols(tcol + 2 * SEC))
             mixed = sum(pv(w, v) for w, v in zip(ws, vs))
             video_ref[:, hcol(col)] = (mixed / total).astype(jnp.bfloat16)
+        span = pl.ds(pl.multiple_of(c * CW, 128), CW)
+        pltpu.make_async_copy(video_ref.at[:, span], video_hbm.at[:, span], lsem.at[4]).start()
 
     relay_x(1)
     relay_t(1)
 
     @functools.partial(lax.fori_loop, 0, CHUNKS, init_val=0)
     def _(c, carry):
-        odd = lax.rem(c, 2)
-        relay_x(jnp.where(odd == 1, c + 2, c + 6), c < jnp.where(odd == 1, 10, 6))
-        relay_t(c + 3, c < CHUNKS - 3)
-
-        @pl.when(jnp.logical_and(odd == 0, c < 6))
+        pl.when(c == AT1)(merge1)
+        relay_t(3, c == AT1)
+        relay_x(jnp.where(c == AT1, 6, c + 6), jnp.logical_or(c == AT1, jnp.logical_and(lax.rem(c, 2) == 0, jnp.logical_and(c > 0, c < 6))))
+
+        @pl.when(jnp.logical_or(c == AT1, jnp.logical_and(lax.rem(c, 2) == 0, jnp.logical_and(c > 0, c < 6))))
         def _():
             for k, cond in crossing:
 
                 @pl.when(cond)
                 def _():
-                    send_halo(k, c + 7)
-
-        pl.when(c == AT1)(merge1)
+                    send_halo(k, jnp.where(c == AT1, 7, c + 7))
+
+        relay_x(c + 2, jnp.logical_and(lax.rem(c, 2) == 1, c < 10))
+        relay_t(c + 3, jnp.logical_and(c >= AT1, c < CHUNKS - 3))
         pl.when(c == AT2)(merge2)
         pl.when(c == CHUNKS - 1)(merge3)
         video(c)
@@ -519,6 +529,7 @@
     chosen = jnp.dot(pick, full[...], preferred_element_type=jnp.float32)
     tout_ref[...] = chosen[:2].astype(jnp.bfloat16)
 
+    pltpu.make_async_copy(video_ref, video_hbm, lsem.at[4]).wait()
     for i in range(1, 8):
         g_copy(i, g).wait_send()
     for part in range(3):
@@ -553,6 +564,9 @@
     whole = pl.BlockSpec(memory_space=pltpu.VMEM)
     hbm = pl.BlockSpec(memory_space=pl.ANY)
     scratch = [
+        vm((2, TCOLS), bf),
+        vm((1, 256), jnp.int32),
+        vm((TILE, D), bf),
         vm((5, TILE, 2 * D), bf),
         vm((TILE, D), bf),
         vm((16, TCOLS // 8), bf),
@@ -575,14 +589,14 @@
         vm((16, D // 2), bf),
         vm((2, 16, HEAD), f32),
         vm((16, D), bf),
-        dma((2,)), dma((8,)), dma((8,)), dma((3, 2, 4)), dma((3, 2, 4)),
+        dma((5,)), dma((8,)), dma((8,)), dma((3, 2, 4)), dma((3, 2, 4)),
         dma((2,)), dma((2,)), dma, dma, dma, dma, dma((4,)), dma((4, CHUNKS, 2)), dma((2,)), dma((7, 4)), dma((7, 4)),
     ]
     video_out, text_out = pl.pallas_call(
         kernel,
         out_shape=(jax.ShapeDtypeStruct((TILE, D), bf), jax.ShapeDtypeStruct((2, D), bf)),
-        in_specs=[hbm, hbm, whole, whole, pl.BlockSpec(memory_space=pltpu.SMEM)],
-        out_specs=(whole, whole),
+        in_specs=[hbm, hbm, hbm, hbm, pl.BlockSpec(memory_space=pltpu.SMEM)],
+        out_specs=(hbm, whole),
         scratch_shapes=scratch,
         compiler_params=pltpu.CompilerParams(
             collective_id=0, has_side_effects=True, vmem_limit_bytes=58 * 2**20

time: 103 us -> 96.3 us (0.935)
  the two profiles are of different devices: /device:TPU:6 before, /device:TPU:31 now
where the time goes in v3:
time: 96.3 us; the launch traced here: 96.1 us
  Pallas kernels  92.2 us (96%)
  local copies, waits for them, and re-layouts  3.26 us (3%)
    pallas_call x1, Pallas kernels, local(): pl.pallas_call(kernel, out_shape=(jax.ShapeDtypeStruct((TILE, D), bf), ja...  92.2 us
    unnamed x4, local copies, waits for them, and re-layouts  3.26 us

profile of v3, /device:TPU:31, one launch (start us, length us, event | category | flops | bytes accessed | tf_op | source)
XLA Modules:
  0.0 96.1 jit_solution(14605505094823492390)
XLA Ops:
  0.6 92.2 %shard_map.68 = (bf16[256,3072]{1,0:T(8,128)(2,1)}, bf16[2,3072]{1,0:T(2,128)(2,1)}) custom-call(bf16[256,3072]{1,0:T(8,128)(2,1)} %bitcast.7, bf16[256,6144]{1,0:T(8,128)(2,1)} %bitcast.6, bf16[2,9216]{1,0:T(2,128)(2,1)} %text_hbm.1, s32[1,256]{1,0:T(1,128)} %bitcast.8, s32[4]{0:T(128)} %bitcast.9), custom_call_target="tpu_custom_call" | custom-call | flops 6000000000 | bytes 10000000 | tf_op jit(solution)/shard_map/pallas_call | solution.py:595
  92.9 0.0 copy-start
  92.9 2.7 %copy.9 = bf16[1,1,256,3072]{3,2,1,0:T(8,128)(2,1)} copy(bf16[1,1,256,3072]{3,2,1,0:T(8,128)(2,1)} %bitcast.5) | data formatting | bytes 3145728
  95.5 0.0 copy-done
  95.5 0.6 copy.10
Async XLA Ops:
  92.9 2.7 %copy-start = (bf16[2,3072]{1,0:T(2,128)(2,1)S(1)}, bf16[2,3072]{1,0:T(2,128)(2,1)}, u32[]{:S(2)}) copy-start(bf16[2,3072]{1,0:T(2,128)(2,1)} %get-tuple-element.9) | copy-start | bytes 36868

commit v4 on v3

--- a/solution.py
+++ b/solution.py
@@ -177,6 +177,7 @@
     send_loop(0, 1, along_x + crossing)
     send_loop(0, FAR_EARLY, [(FAR, has_far)])
     send_loop(1, 2, crossing)
+    send_loop(4, 5, [(FAR, far_cross)])
     send_loop(1, X_EARLY, along_x)
     send_loop(2, CHUNKS, crossing, 2)
 
@@ -301,7 +302,7 @@
     def text_cols(col):
         return T[:, :, :, hcol(col)].reshape(256, HEAD)
 
-    @functools.partial(lax.fori_loop, 0, HALF, init_val=0)
+    @functools.partial(lax.fori_loop, 0, HALF, init_val=0, unroll=2)
     def _(hh, carry):
         col = base + (hh // 6) * TQ + lax.rem(hh, 6) * HEAD
         kcol = core * (D // 2) + hh * HEAD
@@ -348,7 +349,7 @@
         for cp in r1(i, up(y, i)):
             cp.start()
     send_loop(FAR_EARLY, CHUNKS, [(FAR, jnp.logical_and(has_far, jnp.logical_not(far_cross)))])
-    send_loop(4, CHUNKS, [(FAR, far_cross)], 2)
+    send_loop(6, CHUNKS, [(FAR, far_cross)], 2)
 
     step_waits(1, 2)
 
@@ -362,7 +363,7 @@
 
     ST[...] = jnp.zeros_like(ST)
 
-    @functools.partial(lax.fori_loop, 0, HALF, init_val=0)
+    @functools.partial(lax.fori_loop, 0, HALF, init_val=0, unroll=4)
     def _(hh, carry):
         col = base + (hh // 6) * TQ + lax.rem(hh, 6) * HEAD
         sc = qk(T[y, z, :, hcol(col)], text_cols(col + SEC)) + bias2_ref[0:1, :]

time: 96.3 us -> 96.3 us (level)
  no operation moved by 1% of the time
where the time goes in v4:
time: 96.3 us; the launch traced here: 96.1 us
  Pallas kernels  92.2 us (96%)
  local copies, waits for them, and re-layouts  3.26 us (3%)
    pallas_call x1, Pallas kernels, local(): pl.pallas_call(kernel, out_shape=(jax.ShapeDtypeStruct((TILE, D), bf), ja...  92.2 us
    unnamed x4, local copies, waits for them, and re-layouts  3.26 us

profile of v4, /device:TPU:31, one launch (start us, length us, event | category | flops | bytes accessed | tf_op | source)
XLA Modules:
  0.0 96.1 jit_solution(4066204726944399978)
XLA Ops:
  0.6 92.2 %shard_map.68 = (bf16[256,3072]{1,0:T(8,128)(2,1)}, bf16[2,3072]{1,0:T(2,128)(2,1)}) custom-call(bf16[256,3072]{1,0:T(8,128)(2,1)} %bitcast.7, bf16[256,6144]{1,0:T(8,128)(2,1)} %bitcast.6, bf16[2,9216]{1,0:T(2,128)(2,1)} %text_hbm.1, s32[1,256]{1,0:T(1,128)} %bitcast.8, s32[4]{0:T(128)} %bitcast.9), custom_call_target="tpu_custom_call" | custom-call | flops 6000000000 | bytes 10000000 | tf_op jit(solution)/shard_map/pallas_call | solution.py:596
  92.8 0.0 copy-start
  92.8 2.7 %copy.9 = bf16[1,1,256,3072]{3,2,1,0:T(8,128)(2,1)} copy(bf16[1,1,256,3072]{3,2,1,0:T(8,128)(2,1)} %bitcast.5) | data formatting | bytes 3145728
  95.5 0.0 copy-done
  95.5 0.6 copy.10
Async XLA Ops:
  92.8 2.7 %copy-start = (bf16[2,3072]{1,0:T(2,128)(2,1)S(1)}, bf16[2,3072]{1,0:T(2,128)(2,1)}, u32[]{:S(2)}) copy-start(bf16[2,3072]{1,0:T(2,128)(2,1)} %get-tuple-element.9) | copy-start | bytes 36868
